TPU v7x, 256 devices: a whole 4x4x8 slice. The times are simulated.
256 devices in a mesh: dp: 8 (over x, core), expert: 32 (over z, y).
Axes of the slice: x: 4, y: 4, z: 8, core: 2. Of those that a mesh axis runs over, the one named last changes fastest.
Arguments:
- features: bfloat16 [65536, 2048], P(('dp', 'expert')), may hold values from -6 to 6
- expert_ids: int32 [65536, 2], P(('dp', 'expert')), may hold values from 0 to 31, all different within a row; in each aligned block of 256 rows (0 to 255, 256 to 511, ...) at most 32 rows name the same one
- gate_weights: float32 [65536, 2], P(('dp', 'expert')), may hold values from 0.1 to 1
- out_grads: bfloat16 [65536, 2, 1536], P(('dp', 'expert')), may hold values from -6 to 6
Outputs:
- input_factor: float32 [32, 2048, 2048], P('expert', 'dp')
- grad_factor: float32 [32, 1536, 1536], P('expert', 'dp')
Inputs may be any that keep to these rules, and one draw needn't show every extreme that they name: `expert_ids`: each row names 2 different experts. Among the 256 tokens of one device no expert is named by more than 32 rows, a bound that some block reaches.
All inputs are finite; a program needn't handle non-finite values.
Results may differ from a plain program's by a relative error of at most 0.0027.
Values may be sent and summed in bfloat16 or wider, within the bound.
A program may use at most 128 MiB of HBM per device.

v0:
```python
import jax
import jax.numpy as jnp
from jax import lax
from jax.experimental import pallas as pl
from jax.experimental.pallas import tpu as pltpu
from jax.sharding import PartitionSpec as P

MESH = pl.DeviceIdType.MESH
BF = jnp.bfloat16
F32 = jnp.float32

N_DP = 8
N_Z = 8
N_Y = 4
E = 32
CAP = 32
ROWS = E * CAP
W = 512
SUB = 64
SCALE = 1.0 / 1024.0


PR, PC = 32, 128
HALF = N_DP // 2
DIAG = 3


def half_pieces(j):
    return j * HALF + DIAG


def make_panels(nf, ng):
    panels = []
    ub = tb = rb = 0
    for kind, count in (("f", nf), ("g", ng)):
        for j in range(count):
            panels.append(dict(kind=kind, J=j, ub=ub, tb=tb, rb=rb, first=len(panels) - j))
            ub += j + 1
            tb += j
            rb += 2 * half_pieces(j)
    return panels, ub, tb, rb


NF, NG = 4, 3
PANELS, UNITS, TUNITS, PIECES = make_panels(NF, NG)
NP = len(PANELS)
AHEAD = 2


def make_order(first=8.0, every=15.0, hop=1.6, lag=2.5, move_lag=4.0, x_lag=15.0):
    ready = {("land", p, 0): first + every * (p + 1) for p in range(NP)}
    link = now = 0.0
    order = []
    halves = dict.fromkeys(range(NP), 0)
    while ready:
        now = max(now, min(ready.values()))
        op = min(ready, key=lambda o: (ready[o] - (4.0 if o[1] >= 5 else 0.0), o[1], str(o[0]), o[2]))
        del ready[op]
        order.append(op)
        kind, p, h = op
        size = PANELS[p]["J"] + 1
        ring_size = PANELS[p]["J"] + 0.75
        if kind == "land":
            now += 1.3 * size + 3.0
            for h in (0, 1):
                link = max(link, now) + 0.25 * hop * ring_size
                ready[(2, p, h)] = link + lag
        elif kind == "sum":
            now += 0.3 * size + 0.3
            ready[("turn", p, 0)] = now + 0.5 * size + x_lag
        elif kind == "turn":
            now += 0.3
            link = max(link, now) + hop * size
            ready[("out", p, 0)] = link + move_lag
        elif kind == "out":
            now += 0.3 * size + 0.3
            ready[("tile", p, 0)] = now + x_lag + size
        elif kind == "tile":
            now += 0.5 * size
        else:
            now += 0.2 * size + 0.15
            link = max(link, now) + 0.5 * hop * ring_size
            if kind < 4:
                ready[(kind + 1, p, h)] = link + lag
            else:
                halves[p] += 1
                if halves[p] == 2:
                    ready[("sum", p, 0)] = link + lag
    return order


def kernel(
    feats, raw, gates, ids, of, og,
    grads, scaled, panel_f, panel_g, sel, self_f, sb, rb, gram, rsd, rsu, st, ts, tx, tr, tt, td,
    a_send, a_recv, d_send, d_recv, u_send, u_recv,
    raw_sem, x_send, x_recv, z_send, z_recv, m_send, m_recv, e_send, e_recv,
):
    dp = lax.axis_index("dp")
    ex = lax.axis_index("expert")
    z = ex // N_Y
    y = ex % N_Y
    me = dp * N_Y + y

    def plane_peer(r):
        q = (me + r) % E
        return q, (q // N_Y, z * N_Y + q % N_Y)

    def line_peer(r):
        q = (z + r) % N_Z
        return q, (dp, q * N_Y + y)

    down = (dp, ((z + N_Z - 1) % N_Z) * N_Y + y)
    up = (dp, ((z + 1) % N_Z) * N_Y + y)

    raw_copy = pltpu.make_async_copy(raw, grads, raw_sem)
    raw_copy.start()
    barrier = pltpu.get_barrier_semaphore()

    def greet(r, c):
        pl.semaphore_signal(barrier, inc=1, device_id=plane_peer(r)[1], device_id_type=MESH)
        return c

    def greet_line(r, c):
        pl.semaphore_signal(barrier, inc=1, device_id=line_peer(r)[1], device_id_type=MESH)
        return c

    lax.fori_loop(1, E, greet, 0)
    lax.fori_loop(1, N_Z, greet_line, 0)

    tokens = feats.shape[0]
    routes = gates.shape[0]
    pairs = routes * tokens
    idv = jnp.concatenate([ids[k : k + 1, :] for k in range(routes)], axis=1)

    def iota(shape, dim):
        return lax.broadcasted_iota(jnp.int32, shape, dim)

    def ones_where(m):
        return jnp.where(m, 1.0, 0.0)

    hot = ones_where(iota((E, pairs), 0) == idv)
    tri = ones_where(iota((pairs, pairs), 0) < iota((pairs, pairs), 1)).astype(BF)
    earlier = jnp.dot(hot.astype(BF), tri, preferred_element_type=F32)
    pos = jnp.sum(earlier * hot, axis=0, keepdims=True)
    target = idv * CAP + pos.astype(jnp.int32)
    chunk = 128

    def select_tokens(i, c):
        r0 = pl.multiple_of(i * chunk, chunk)
        m = ones_where(iota((chunk, pairs), 0) + r0 == target)
        both = sum(m[:, k * tokens : (k + 1) * tokens] for k in range(routes))
        self_f[pl.ds(r0, chunk), :] = both.astype(BF)
        return c

    lax.fori_loop(0, ROWS // chunk, select_tokens, 0)

    def select_pairs(i, c):
        r0 = pl.multiple_of(i * chunk, chunk)
        sel[pl.ds(r0, chunk), :] = ones_where(iota((chunk, pairs), 0) + r0 == target).astype(BF)
        return c

    def scale_grads():
        raw_copy.wait()
        weights = [jnp.broadcast_to(gates[k : k + 1, :], (128, tokens)).T for k in range(routes)]
        for i in range(grads.shape[2] // 128):
            lanes = slice(i * 128, (i + 1) * 128)
            for k in range(routes):
                v = grads[:, k, lanes].astype(F32) * weights[k]
                scaled[k * tokens : (k + 1) * tokens, lanes] = v.astype(BF)

    def gather_columns(pan, ref, b):
        count = NG if pan["kind"] == "g" else NF
        at = [((b + i) * count + pan["J"]) * SUB for i in (0, 1)]
        return [ref[:, pl.ds(a, SUB)] for a in at]

    def arrange(p):
        pan = PANELS[p]
        src, dst = (feats, panel_f) if pan["kind"] == "f" else (scaled, panel_g)
        for m in range(N_DP // 2):
            lanes = slice(2 * SUB * m, 2 * SUB * (m + 1))
            dst[:, lanes] = jnp.concatenate(gather_columns(pan, src, 2 * m), axis=1)

    def build(p):
        pan = PANELS[p]
        arrange(p)
        src = panel_f if pan["kind"] == "f" else panel_g
        pick = self_f if pan["kind"] == "f" else sel

        def one(i, c):
            r0 = pl.multiple_of(i * 256, 256)
            v = jnp.dot(pick[pl.ds(r0, 256), :], src[...], preferred_element_type=F32)
            sb[pl.ds(pl.multiple_of(p * ROWS + r0, 256), 256), :] = v.astype(BF)
            return c

        lax.fori_loop(0, ROWS // 256, one, 0)
        own = pl.multiple_of(p * ROWS + me * CAP, CAP)
        rb[pl.ds(own, CAP), :] = sb[pl.ds(own, CAP), :]

    def push(p):
        def one(r, c):
            q, dev = plane_peer(r)
            pltpu.make_async_remote_copy(
                src_ref=sb.at[pl.ds(pl.multiple_of(p * ROWS + q * CAP, CAP), CAP), :],
                dst_ref=rb.at[pl.ds(pl.multiple_of(p * ROWS + me * CAP, CAP), CAP), :],
                send_sem=a_send.at[p],
                recv_sem=a_recv.at[p],
                device_id=dev,
                device_id_type=MESH,
            ).start()
            return c

        lax.fori_loop(1, E, one, 0)

    def wait_rows(ref, rows, sem):
        v = ref.at[pl.ds(0, rows), :]
        pltpu.make_async_copy(v, v, sem).wait()

    def compute(p):
        pan = PANELS[p]
        f0 = pan["first"]

        def one(i, c):
            k = i // 2
            h = i % 2
            a = rb[pl.ds(p * ROWS, ROWS), pl.ds(pl.multiple_of(h * 256, 256), 256)]
            b = rb[pl.ds(pl.multiple_of((f0 + k) * ROWS, ROWS), ROWS), :]
            v = lax.dot_general(a, b, (((0,), (0,)), ((), ())), preferred_element_type=F32)
            gram[pl.ds(pl.multiple_of((pan["ub"] + k) * W + h * 256, 256), 256), :] = v
            return c

        lax.fori_loop(0, 2 * (pan["J"] + 1), one, 0)

    def piece(pan, k, s, b):
        r = (pan["ub"] + k) * W + b * SUB + (s % 2) * PR
        lanes = pl.ds(pl.multiple_of((s // 2) * PC, PC), PC)
        return gram[pl.ds(pl.multiple_of(r, PR), PR), lanes]

    def seg(pan, t, h, k=0, i=0):
        return (t * PIECES + pan["rb"] + h * half_pieces(pan["J"]) + k * HALF + i) * PR

    def height(pan):
        return half_pieces(pan["J"]) * PR

    def remote(src, dst, ss, rs, dev):
        return pltpu.make_async_remote_copy(
            src_ref=src, dst_ref=dst, send_sem=ss, recv_sem=rs, device_id=dev, device_id_type=MESH
        )

    def ring(p, t, way, h):
        pan = PANELS[p]
        buf, ss, rs, dev = (
            (rsd, d_send, d_recv, down) if way == "d" else (rsu, u_send, u_recv, up)
        )
        n = height(pan)
        if t == 1:
            src = st.at[pl.ds(seg(pan, 0, h), n), :]
        else:
            src = buf.at[pl.ds(seg(pan, t - 2, h), n), :]
        dst = buf.at[pl.ds(seg(pan, t - 1, h), n), :]
        i = (p * 4 + t - 1) * 2 + h
        return remote(src, dst, ss.at[i], rs.at[i], dev)

    def over(pan, h, s, fn):
        def one(k, c):
            for i in range(HALF):
                fn(k, i, h * HALF + i)
            return c

        lax.fori_loop(0, pan["J"], one, 0)
        for i in range(DIAG):
            fn(pan["J"], i, (s // 2 * 2 + h * DIAG + i) % N_DP)

    def far(h):
        return "d" if h == 0 else "u"

    def ring_rows(pan, t, h, k, i):
        return pl.ds(pl.multiple_of(seg(pan, t, h, k, i), PR), PR)

    def step1(p):
        pan = PANELS[p]
        s = (z + 4) % N_Z
        for h in (0, 1):

            def one(k, i, b):
                st[ring_rows(pan, 0, h, k, i), :] = piece(pan, k, s, b).astype(BF)

            over(pan, h, s, one)
            ring(p, 1, far(h), h).start()

    def step(p, t, h):
        pan = PANELS[p]
        order = ("d", "u") if far(h) == "u" else ("u", "d")
        for way in order:
            buf = rsd if way == "d" else rsu
            dist = 5 - t
            s = (z + N_Z - dist) % N_Z if way == "d" else (z + dist) % N_Z
            fresh = t == 2 and way != far(h)
            if not fresh:
                ring(p, t - 1, way, h).wait_recv()

            def one(k, i, b):
                r = ring_rows(pan, t - 2, h, k, i)
                own = piece(pan, k, s, b)
                if not fresh:
                    own = own + buf[r, :].astype(F32)
                buf[r, :] = own.astype(BF)

            over(pan, h, s, one)
            ring(p, t, way, h).start()

    def slot(pan, q, k=0):
        return pan["ub"] * N_DP + q * (pan["J"] + 1) + k

    def slots(pan, q, count):
        return pl.ds(slot(pan, q), count)

    def ringed(b, owner):
        return (b // 2 + N_DP // 2 - owner // 2) % (N_DP // 2) < DIAG

    def by_count(pan, has, fn):
        @pl.when(has)
        def _():
            fn(pan["J"] + 1)

        if pan["J"] > 0:

            @pl.when(jnp.logical_not(has))
            def _():
                fn(pan["J"])

    def place(pan, q, count):
        return (
            pl.ds(pan["ub"], count),
            pl.ds(pl.multiple_of((q % 2) * PR, PR), PR),
            pl.ds(pl.multiple_of((q // 2) * PC, PC), PC),
        )

    def finish(p):
        pan = PANELS[p]
        for h in (0, 1):
            ring(p, 4, "d", h).wait_recv()
            ring(p, 4, "u", h).wait_recv()

            def one(k, i, b):
                r = ring_rows(pan, 3, h, k, i)
                v = piece(pan, k, z, b) + rsd[r, :].astype(F32) + rsu[r, :].astype(F32)
                ts[slot(pan, b, k)] = v.astype(BF)

            over(pan, h, z, one)

        def one_peer(r, c):
            b = (dp + r) % N_DP

            def send(count):
                remote(
                    ts.at[slots(pan, b, count)],
                    tx.at[slots(pan, dp, count)],
                    x_send.at[p],
                    x_recv.at[p],
                    (b, ex),
                ).start()

            by_count(pan, ringed(b, z), send)
            return c

        lax.fori_loop(1, N_DP, one_peer, 0)

        def keep(count):
            tx[slots(pan, dp, count)] = ts[slots(pan, dp, count)]

        by_count(pan, ringed(dp, z), keep)

    def turn(p):
        pan = PANELS[p]
        wait_equal(pan, x_recv.at[p])

        def move(count):
            def one_peer(r, c):
                q, dev = line_peer(r)
                remote(
                    tx.at[slots(pan, q, count)],
                    tr.at[place(pan, z, count)],
                    z_send.at[p],
                    z_recv.at[p],
                    dev,
                ).start()
                return c

            lax.fori_loop(1, N_Z, one_peer, 0)
            tr[place(pan, z, count)] = tx[slots(pan, z, count)]

        by_count(pan, ringed(dp, z), move)

    def wait_equal(pan, sem):
        by_count(pan, ringed(dp, z), lambda count: wait_slots((N_DP - 1) * count, sem))

    def wait_mixed(pan, sem):
        most = (N_DP - 1) * (pan["J"] + 1)

        @pl.when(ringed(dp, z))
        def _():
            wait_slots(most - (N_DP - 2 * DIAG), sem)

        @pl.when(jnp.logical_not(ringed(dp, z)))
        def _():
            wait_slots(most - (N_DP - 2 * DIAG) + 1, sem)

    def wait_slots(count, sem):
        v = ts.at[pl.ds(0, count)]
        pltpu.make_async_copy(v, v, sem).wait()

    def put(pan, row, col, v):
        out, count = (of, NF) if pan["kind"] == "f" else (og, NG)
        v = v.astype(BF)
        for b in range(N_DP):
            c = (b * count + col) * SUB
            out[0, pl.ds(row * SUB, SUB), pl.ds(c, SUB)] = v[:, b * SUB : (b + 1) * SUB]

    def tile_slot(pan, b):
        return pan["tb"] * N_DP + b * pan["J"]

    def wait_tiles(j, sem):
        v = tt.at[pl.ds(0, (N_DP - 1) * j)]
        pltpu.make_async_copy(v, v, sem).wait()

    def spread(p):
        pan = PANELS[p]
        j = pan["J"]
        wait_mixed(pan, z_recv.at[p])
        if j > 0:
            mine = pl.ds(pan["ub"], j)
            dst = pl.ds(tile_slot(pan, dp), j)

            def one(r, c):
                b = (dp + r) % N_DP
                lanes = pl.ds(pl.multiple_of((b // 2) * 128, 128), 128)
                remote(
                    tr.at[mine, :, lanes], tt.at[dst], m_send.at[p], m_recv.at[p], (b, ex)
                ).start()
                return c

            lax.fori_loop(1, N_DP, one, 0)
            own_lanes = pl.ds(pl.multiple_of((dp // 2) * 128, 128), 128)
            tt[dst] = tr[mine, :, own_lanes]
        for i in (0, 1):
            e_copy(p, i).start()
        for k in range(j):
            put(pan, j, k, tr[pan["ub"] + k])

    def e_copy(p, i):
        pan = PANELS[p]
        m = (dp // 2 + N_DP // 2 - 1) % (N_DP // 2)
        lanes = pl.ds(pl.multiple_of(m * 128, 128), 128)
        return remote(
            tr.at[pan["ub"] + pan["J"], :, lanes],
            td.at[p * 2 + dp % 2],
            e_send.at[p],
            e_recv.at[p],
            (m * 2 + i, ex),
        )

    def wait_diag(sem):
        v = td.at[pl.ds(0, 2)]
        pltpu.make_async_copy(v, v, sem).wait()

    def collect(p):
        pan = PANELS[p]
        j = pan["J"]
        off = (dp % 2) * SUB
        pick = lax.broadcasted_iota(jnp.int32, (SUB, 128), 1) == (
            lax.broadcasted_iota(jnp.int32, (SUB, 128), 0) + off
        )
        pick = jnp.where(pick, 1.0, 0.0).astype(BF)
        wait_diag(e_recv.at[p])
        tiles = jnp.concatenate([td[p * 2], td[p * 2 + 1]], axis=0)
        v = lax.dot_general(pick, tiles, (((1,), (1,)), ((), ())), preferred_element_type=F32)
        parts = []
        for m in range(N_DP // 2):
            have = tr[pan["ub"] + j, :, m * 128 : (m + 1) * 128].astype(F32)
            parts.append(jnp.where((dp // 2 + 1) % (N_DP // 2) == m, v, have))
        put(pan, j, j, jnp.concatenate(parts, axis=1))
        if j > 0:
            wait_tiles(j, m_recv.at[p])
        for k in range(j):
            parts = [tt[tile_slot(pan, b) + k] for b in range(N_DP)]
            tiles = jnp.concatenate(parts, axis=0)
            v = lax.dot_general(pick, tiles, (((1,), (1,)), ((), ())), preferred_element_type=F32)
            put(pan, k, j, v)

    def land(p):
        wait_rows(rb, (E - 1) * CAP, a_recv.at[p])

    build(0)
    pl.semaphore_wait(barrier, E - 1 + N_Z - 1)
    push(0)
    for p in range(1, AHEAD):
        build(p)
        push(p)
    lax.fori_loop(0, ROWS // chunk, select_pairs, 0)
    scale_grads()

    def front(p):
        land(p)
        if p + AHEAD < NP:
            build(p + AHEAD)
            push(p + AHEAD)
        compute(p)
        step1(p)

    for kind, p, h in make_order():
        if kind == "land":
            front(p)
        elif kind == "sum":
            finish(p)
        elif kind == "turn":
            turn(p)
        elif kind == "out":
            spread(p)
        elif kind == "tile":
            collect(p)
        else:
            step(p, kind, h)

    for p in range(NP):
        wait_rows(sb, (E - 1) * CAP, a_send.at[p])
        for h in (0, 1):
            ring(p, 1, far(h), h).wait_send()
            for t in (2, 3, 4):
                ring(p, t, "d", h).wait_send()
                ring(p, t, "u", h).wait_send()
        wait_mixed(PANELS[p], x_send.at[p])
        wait_equal(PANELS[p], z_send.at[p])
        j = PANELS[p]["J"]
        wait_diag(e_send.at[p])
        if j > 0:
            wait_tiles(j, m_send.at[p])


def finalize(f_in, g_in, f_out, g_out):
    f_out[...] = f_in[...].astype(F32) * SCALE
    g_out[...] = g_in[...].astype(F32) * SCALE


def per_device(features, expert_ids, gate_weights, out_grads):
    tokens, width = features.shape
    routes, hidden = out_grads.shape[1:]
    pairs = routes * tokens
    nf, ng = width // W, hidden // W
    vm = pl.BlockSpec(memory_space=pltpu.VMEM)
    hbm = pl.BlockSpec(memory_space=pl.ANY)
    dma = pltpu.SemaphoreType.DMA
    of, og = pl.pallas_call(
        kernel,
        out_shape=(
            jax.ShapeDtypeStruct((1, nf * SUB, width), BF),
            jax.ShapeDtypeStruct((1, ng * SUB, hidden), BF),
        ),
        in_specs=[vm, hbm, vm, vm],
        out_specs=(vm, vm),
        scratch_shapes=[
            pltpu.VMEM((tokens, routes, hidden), BF),
            pltpu.VMEM((pairs, hidden), BF),
            pltpu.VMEM((tokens, W), BF),
            pltpu.VMEM((pairs, W), BF),
            pltpu.VMEM((ROWS, pairs), BF),
            pltpu.VMEM((ROWS, tokens), BF),
            pltpu.VMEM((NP * ROWS, W), BF),
            pltpu.VMEM((NP * ROWS, W), BF),
            pltpu.VMEM((UNITS * W, W), F32),
            pltpu.VMEM((4 * PIECES * PR, PC), BF),
            pltpu.VMEM((4 * PIECES * PR, PC), BF),
            pltpu.VMEM((PIECES * PR, PC), BF),
            pltpu.VMEM((UNITS * N_DP, PR, PC), BF),
            pltpu.VMEM((UNITS * N_DP, PR, PC), BF),
            pltpu.VMEM((UNITS, SUB, W), BF),
            pltpu.VMEM((TUNITS * N_DP, SUB, 128), BF),
            pltpu.VMEM((NP * 2, SUB, 128), BF),
            dma((NP,)),
            dma((NP,)),
            dma((NP * 8,)),
            dma((NP * 8,)),
            dma((NP * 8,)),
            dma((NP * 8,)),
            dma,
            dma((NP,)),
            dma((NP,)),
            dma((NP,)),
            dma((NP,)),
            dma((NP,)),
            dma((NP,)),
            dma((NP,)),
            dma((NP,)),
        ],
        compiler_params=pltpu.CompilerParams(
            collective_id=0, has_side_effects=True, vmem_limit_bytes=60 * 1024 * 1024
        ),
        cost_estimate=pl.CostEstimate(
            flops=9_000_000_000, bytes_accessed=8_000_000, transcendentals=0
        ),
    )(features, out_grads, gate_weights.T, expert_ids.T)
    steps = 4

    def block(x):
        return pl.BlockSpec((1, x.shape[1] // steps, x.shape[2]), lambda i: (0, i, 0))

    return pl.pallas_call(
        finalize,
        grid=(steps,),
        out_shape=tuple(jax.ShapeDtypeStruct(x.shape, F32) for x in (of, og)),
        in_specs=[block(of), block(og)],
        out_specs=(block(of), block(og)),
    )(of, og)


def solution(mesh):
    in_specs = (
        P(("dp", "expert"), None),
        P(("dp", "expert"), None),
        P(("dp", "expert"), None),
        P(("dp", "expert"), None, None),
    )
    out_specs = (P("expert", "dp", None), P("expert", "dp", None))
    return jax.shard_map(
        per_device, mesh=mesh, in_specs=in_specs, out_specs=out_specs, check_vma=False
    )
```

profile of v0, /device:TPU:1, one launch (start us, length us, event | category | flops | bytes accessed | tf_op | source)
XLA Modules:
  0.0 168.6 jit_solution(15888059213420363390)
XLA Ops:
  0.6 164.1 %shard_map.59 = (bf16[1,256,2048]{2,1,0:T(8,128)(2,1)}, bf16[1,192,1536]{2,1,0:T(8,128)(2,1)}) custom-call(bf16[256,2048]{1,0:T(8,128)(2,1)} %feats.1, bf16[256,2,1536]{2,1,0:T(2,128)(2,1)} %raw.1, f32[2,256]{1,0:T(2,128)} %bitcast.2, s32[2,256]{1,0:T(2,128)} %bitcast.3), custom_call_target="tpu_custom_call" | custom-call | flops 8999999488 | bytes 8000000 | tf_op jit(solution)/shard_map/pallas_call | solution.py:552
  164.7 3.9 %shard_map.60 = (f32[1,256,2048]{2,1,0:T(8,128)}, f32[1,192,1536]{2,1,0:T(8,128)}) custom-call(bf16[1,256,2048]{2,1,0:T(8,128)(2,1)} %get-tuple-element.4.f_in, bf16[1,192,1536]{2,1,0:T(8,128)(2,1)} %get-tuple-element.5.g_in), custom_call_target="tpu_custom_call" | custom-call | tf_op jit(solution)/shard_map/pallas_call | solution.py:606
where the time goes:
time: 169 us
  Pallas kernels  168 us (99%)
    pallas_call x1, Pallas kernels, per_device(): pl.pallas_call(kernel, out_shape=(jax.ShapeDtypeStruct((1, nf * SUB, widt...  164 us
    pallas_call x1, Pallas kernels, per_device(): pl.pallas_call(finalize, grid=(steps,), out_shape=tuple((jax.ShapeDtypeSt...  3.86 us

commit v1 on v0

--- a/solution.py
+++ b/solution.py
@@ -498,14 +498,16 @@
         push(p)
     lax.fori_loop(0, ROWS // chunk, select_pairs, 0)
     scale_grads()
+    build(AHEAD)
 
     def front(p):
         land(p)
         if p + AHEAD < NP:
-            build(p + AHEAD)
             push(p + AHEAD)
         compute(p)
         step1(p)
+        if p + AHEAD + 1 < NP:
+            build(p + AHEAD + 1)
 
     for kind, p, h in make_order():
         if kind == "land":

time: 169 us -> 167 us (0.988)
  no operation moved by 1% of the time
where the time goes in v1:
time: 167 us
  Pallas kernels  167 us (100%)
    pallas_call x1, Pallas kernels, per_device(): pl.pallas_call(kernel, out_shape=(jax.ShapeDtypeStruct((1, nf * SUB, widt...  163 us
    pallas_call x1, Pallas kernels, per_device(): pl.pallas_call(finalize, grid=(steps,), out_shape=tuple((jax.ShapeDtypeSt...  3.86 us

profile of v1, /device:TPU:1, one launch (start us, length us, event | category | flops | bytes accessed | tf_op | source)
XLA Modules:
  0.0 167.1 jit_solution(6903459280009157809)
XLA Ops:
  0.6 162.6 %shard_map.59 = (bf16[1,256,2048]{2,1,0:T(8,128)(2,1)}, bf16[1,192,1536]{2,1,0:T(8,128)(2,1)}) custom-call(bf16[256,2048]{1,0:T(8,128)(2,1)} %feats.1, bf16[256,2,1536]{2,1,0:T(2,128)(2,1)} %raw.1, f32[2,256]{1,0:T(2,128)} %bitcast.2, s32[2,256]{1,0:T(2,128)} %bitcast.3), custom_call_target="tpu_custom_call" | custom-call | flops 8999999488 | bytes 8000000 | tf_op jit(solution)/shard_map/pallas_call | solution.py:554
  163.3 3.9 %shard_map.60 = (f32[1,256,2048]{2,1,0:T(8,128)}, f32[1,192,1536]{2,1,0:T(8,128)}) custom-call(bf16[1,256,2048]{2,1,0:T(8,128)(2,1)} %get-tuple-element.4.f_in, bf16[1,192,1536]{2,1,0:T(8,128)(2,1)} %get-tuple-element.5.g_in), custom_call_target="tpu_custom_call" | custom-call | tf_op jit(solution)/shard_map/pallas_call | solution.py:608
